TPU v7x, 32 devices: a whole 2x2x4 slice. The times are simulated.
32 devices in a mesh: dp: 8 (over z, y), shard: 4 (over x, core).
Axes of the slice: x: 2, y: 2, z: 4, core: 2. Of those that a mesh axis runs over, the one named last changes fastest.
Arguments:
- tokens: bfloat16 [4, 1024, 960], P('shard', 'dp'), may hold values from -6 to 6
- cotangent: bfloat16 [4, 1024, 960], P('shard', 'dp'), may hold values from -6 to 6
- seq_lengths: int32 [4, 2], P('shard'), may hold values from 1 to 512, as said below
- block_slot: int32 [4, 8], P('shard'), may hold values from 0 to 7, as said below
- qkv_master: float32 [960, 1600], P('shard', 'dp'), may hold values from -0.1875 to 0.1875
- qkv_first: float32 [960, 1600], P('shard', 'dp'), may hold values from -6 to 6
- qkv_second: float32 [960, 1600], P('shard', 'dp'), may hold values from 3.19488 to 51.6096
- out_master: float32 [960, 960], P('shard', 'dp'), may hold values from -0.75 to 0.75
- out_first: float32 [960, 960], P('shard', 'dp'), may hold values from -6 to 6
- out_second: float32 [960, 960], P('shard', 'dp'), may hold values from 3.19488 to 51.6096
- gate_up_master: float32 [960, 5120], P('shard', 'dp'), may hold values from -0.1875 to 0.1875
- gate_up_first: float32 [960, 5120], P('shard', 'dp'), may hold values from -6 to 6
- gate_up_second: float32 [960, 5120], P('shard', 'dp'), may hold values from 7.18848 to 116.1216
- down_master: float32 [2560, 960], P('shard', 'dp'), may hold values from -0.125 to 0.125
- down_first: float32 [2560, 960], P('shard', 'dp'), may hold values from -6 to 6
- down_second: float32 [2560, 960], P('shard', 'dp'), may hold values from 7.18848 to 116.1216
- gains_master: float32 [2, 960], replicated, may hold values from 0.5 to 1.5
- gains_first: float32 [2, 960], replicated, may hold values from -24 to 24
- gains_second: float32 [2, 960], replicated, may hold values from 39.0144 to 632.832
Outputs:
- layer_out: bfloat16 [4, 1024, 960], P('shard', 'dp')
- input_grad: bfloat16 [4, 1024, 960], P('shard', 'dp')
- qkv_grad: float32 [960, 1600], P('shard', 'dp')
- qkv_first_new: float32 [960, 1600], P('shard', 'dp')
- qkv_second_new: float32 [960, 1600], P('shard', 'dp')
- qkv_new: float32 [960, 1600], P('shard', 'dp')
- out_grad: float32 [960, 960], P('shard', 'dp')
- out_first_new: float32 [960, 960], P('shard', 'dp')
- out_second_new: float32 [960, 960], P('shard', 'dp')
- out_new: float32 [960, 960], P('shard', 'dp')
- gate_up_grad: float32 [960, 5120], P('shard', 'dp')
- gate_up_first_new: float32 [960, 5120], P('shard', 'dp')
- gate_up_second_new: float32 [960, 5120], P('shard', 'dp')
- gate_up_new: float32 [960, 5120], P('shard', 'dp')
- down_grad: float32 [2560, 960], P('shard', 'dp')
- down_first_new: float32 [2560, 960], P('shard', 'dp')
- down_second_new: float32 [2560, 960], P('shard', 'dp')
- down_new: float32 [2560, 960], P('shard', 'dp')
- gains_grad: float32 [2, 960], replicated
- gains_first_new: float32 [2, 960], replicated
- gains_second_new: float32 [2, 960], replicated
- gains_new: float32 [2, 960], replicated
Inputs may be any that keep to these rules, and one draw needn't show every extreme that they name: `seq_lengths`: row s holds the lengths of the 2 sequences of group s; they sum to 768 and the largest is exactly 512. Each row is a permutation: logical block b of group s is stored in slot block_slot[s, b].
All inputs are finite; a program needn't handle non-finite values.
Results may differ from a plain program's by a relative error of at most 0.013.
Values may be sent and summed in bfloat16 or wider, within the bound.
A program may use at most 192 MiB of HBM per device.

v0:
```python
import math

import jax
import jax.numpy as jnp
from jax import lax
from jax.sharding import PartitionSpec as P

HEADS = 15
KV_HEADS = 5
HEAD = 64
FF = 2560
BLOCK = 128
KBLK = 16
STEP = 10


NORM_EPS = 1e-05
MATRIX_RATE = 0.06
GAIN_RATE = 0.4
WEIGHT_DECAY = 0.1


def layout(lengths, blocks_total):
    seq_count = lengths.shape[0]
    counts = (lengths + BLOCK - 1) // BLOCK
    block_ends = jnp.cumsum(counts)
    block_starts = block_ends - counts
    row_index = jnp.arange(blocks_total * BLOCK, dtype=jnp.int32)
    member = jnp.sum(
        (block_ends[None, :] <= (row_index // BLOCK)[:, None]).astype(jnp.int32), axis=1
    )
    choose = (member[:, None] == jnp.arange(seq_count, dtype=jnp.int32)[None, :]).astype(jnp.int32)
    offset = row_index - BLOCK * jnp.sum(choose * block_starts[None, :], axis=1)
    length_row = jnp.sum(choose * lengths[None, :], axis=1)
    usable = (member < seq_count) & (offset < length_row)
    labels = jnp.where(usable, member, seq_count + row_index)
    position = jnp.where(usable, offset, 0)
    return (labels, position, usable)


def rope_tables(position):
    frequency = jnp.exp(
        jnp.arange(HEAD // 2, dtype=jnp.float32) * (-2.0 * math.log(10000.0) / HEAD)
    )
    angle_grid = position.astype(jnp.float32)[:, None] * frequency[None, :]
    return (jnp.cos(angle_grid)[:, None, :], jnp.sin(angle_grid)[:, None, :])


def rotate(vectors, cosine_table, sine_table):
    middle = HEAD // 2
    lower_half = vectors[..., :middle]
    upper_half = vectors[..., middle:]
    return jnp.concatenate(
        [
            lower_half * cosine_table - upper_half * sine_table,
            upper_half * cosine_table + lower_half * sine_table,
        ],
        axis=-1,
    )


def unrotate(grads, cosine_table, sine_table):
    middle = HEAD // 2
    lower_half = grads[..., :middle]
    upper_half = grads[..., middle:]
    return jnp.concatenate(
        [
            lower_half * cosine_table + upper_half * sine_table,
            upper_half * cosine_table - lower_half * sine_table,
        ],
        axis=-1,
    )


def rms_back(source, scale, gain, upstream):
    weighted = gain * upstream
    grad_in = scale * weighted - source * scale**3 * jnp.mean(
        weighted * source, axis=-1, keepdims=True
    )
    return (grad_in, jnp.sum(upstream * source * scale, axis=0))


def scores_for(query_group, key_group, allowed):
    raw_scores = (
        jnp.einsum("nqrd,nkd->nrqk", query_group, key_group, preferred_element_type=jnp.float32)
        * 0.125
    )
    return jnp.where(allowed[:, None], raw_scores, -1e30)


def adamw(master, grad, first, second, rate, decay):
    first_new = 0.9 * first + 0.1 * grad
    second_new = 0.95 * second + 0.05 * grad * grad
    update = first_new / (1.0 - 0.9**STEP) / (jnp.sqrt(second_new / (1.0 - 0.95**STEP)) + 1e-08)
    return (grad, first_new, second_new, master - rate * (update + decay * master))


def body(
    tokens,
    cotangent,
    seq_lengths,
    block_slot,
    qkv_master,
    qkv_first,
    qkv_second,
    out_master,
    out_first,
    out_second,
    gate_up_master,
    gate_up_first,
    gate_up_second,
    down_master,
    down_first,
    down_second,
    gains_master,
    gains_first,
    gains_second,
):
    lengths = seq_lengths[0]
    placing = block_slot[0]
    blocks_total = placing.shape[0]
    window = min(KBLK, blocks_total // 2)
    rows_local = tokens.shape[1]
    local_blocks = rows_local // BLOCK
    grouped = HEADS // KV_HEADS
    width_q = HEADS * HEAD
    width_kv = KV_HEADS * HEAD
    data_count = lax.axis_size("dp")
    owner_count = lax.axis_size("shard")
    qkv_low = qkv_master.astype(jnp.bfloat16)
    out_low = out_master.astype(jnp.bfloat16)
    gate_up_low = gate_up_master.astype(jnp.bfloat16)
    down_low = down_master.astype(jnp.bfloat16)
    qkv_cols, out_cols, gate_up_cols, down_cols = (
        lax.all_gather(qkv_low, "dp", axis=1, tiled=True),
        lax.all_gather(out_low, "dp", axis=1, tiled=True),
        lax.all_gather(gate_up_low, "dp", axis=1, tiled=True),
        lax.all_gather(down_low, "dp", axis=1, tiled=True),
    )
    qkv_weight, out_weight, gate_up_weight, down_weight = (
        lax.all_gather(qkv_cols, "shard", axis=0, tiled=True),
        lax.all_gather(out_cols, "shard", axis=0, tiled=True),
        lax.all_gather(gate_up_cols, "shard", axis=0, tiled=True),
        lax.all_gather(down_cols, "shard", axis=0, tiled=True),
    )
    labels_all, position_all, usable_all = layout(lengths, blocks_total)
    slot_index = jnp.arange(blocks_total, dtype=jnp.int32)
    local_slots = lax.axis_index("dp") * local_blocks + jnp.arange(local_blocks, dtype=jnp.int32)
    own_logical = jnp.sum(
        jnp.where(placing[None, :] == local_slots[:, None], slot_index[None, :], 0), axis=1
    )
    labels_table = labels_all.reshape(blocks_total, BLOCK)
    query_labels = jnp.take(labels_table, own_logical, axis=0)
    query_position = jnp.take(
        position_all.reshape(blocks_total, BLOCK), own_logical, axis=0
    ).reshape(rows_local)
    usable = (
        jnp.take(usable_all.reshape(blocks_total, BLOCK), own_logical, axis=0)
        .reshape(rows_local, 1)
        .astype(jnp.float32)
    )
    within = jnp.arange(BLOCK, dtype=jnp.int32)
    key_logical = own_logical[:, None] - (window - 1) + jnp.arange(window, dtype=jnp.int32)[None, :]
    key_present = key_logical >= 0
    key_clipped = jnp.maximum(key_logical, 0)
    key_slots = jnp.take(placing, key_clipped)
    key_labels = jnp.where(
        key_present[:, :, None], jnp.take(labels_table, key_clipped, axis=0), -1
    ).reshape(local_blocks, window * BLOCK)
    key_order = (key_logical[:, :, None] * BLOCK + within[None, None, :]).reshape(
        local_blocks, window * BLOCK
    )
    query_order = own_logical[:, None] * BLOCK + within[None, :]
    allowed = (query_labels[:, :, None] == key_labels[:, None, :]) & (
        key_order[:, None, :] <= query_order[:, :, None]
    )
    source = tokens[0].astype(jnp.float32)
    scale_first = lax.rsqrt(jnp.mean(source * source, axis=-1, keepdims=True) + NORM_EPS)
    normed_first = (source * scale_first * gains_master[0]).astype(jnp.bfloat16)
    projected = jnp.dot(normed_first, qkv_weight, preferred_element_type=jnp.float32)
    cosine_table, sine_table = rope_tables(query_position)
    queries = rotate(
        projected[:, :width_q].reshape(rows_local, HEADS, HEAD), cosine_table, sine_table
    ).astype(jnp.bfloat16)
    keys_rotated = rotate(
        projected[:, width_q : width_q + width_kv].reshape(rows_local, KV_HEADS, HEAD),
        cosine_table,
        sine_table,
    ).astype(jnp.bfloat16)
    values_local = projected[:, width_q + width_kv :].astype(jnp.bfloat16)
    keys_values = jnp.concatenate(
        [keys_rotated.reshape(rows_local, width_kv), values_local], axis=1
    )
    gathered = lax.all_gather(keys_values, "dp", axis=0, tiled=True)
    window_rows = jnp.take(
        gathered.reshape(blocks_total, BLOCK, 2 * width_kv), key_slots, axis=0
    ).reshape(local_blocks, window * BLOCK, 2 * width_kv)
    query_blocks = queries.reshape(local_blocks, BLOCK, KV_HEADS, grouped, HEAD)
    mixed_parts = []
    lse_parts = []
    for group_index in range(KV_HEADS):
        query_group = query_blocks[:, :, group_index]
        key_group = window_rows[:, :, group_index * HEAD : (group_index + 1) * HEAD]
        value_group = window_rows[
            :, :, width_kv + group_index * HEAD : width_kv + (group_index + 1) * HEAD
        ]
        scores = scores_for(query_group, key_group, allowed)
        top_score = jnp.max(scores, axis=-1, keepdims=True)
        shifted = jnp.exp(scores - top_score)
        totals = jnp.sum(shifted, axis=-1, keepdims=True)
        weights_low = (shifted / totals).astype(jnp.bfloat16)
        mixed_parts.append(
            jnp.einsum(
                "nrqk,nkd->nqrd", weights_low, value_group, preferred_element_type=jnp.float32
            )
        )
        lse_parts.append(top_score + jnp.log(totals))
    attended = jnp.stack(mixed_parts, axis=2).reshape(rows_local, width_q).astype(jnp.bfloat16)
    hidden_state = source + jnp.dot(attended, out_weight, preferred_element_type=jnp.float32)
    scale_second = lax.rsqrt(
        jnp.mean(hidden_state * hidden_state, axis=-1, keepdims=True) + NORM_EPS
    )
    normed_second = (hidden_state * scale_second * gains_master[1]).astype(jnp.bfloat16)
    gate_up = jnp.dot(normed_second, gate_up_weight, preferred_element_type=jnp.float32)
    gate_part = gate_up[:, :FF]
    up_part = gate_up[:, FF:]
    sigmoid_gate = jax.nn.sigmoid(gate_part)
    silu_gate = gate_part * sigmoid_gate
    activated = (silu_gate * up_part).astype(jnp.bfloat16)
    layer_out = (
        (hidden_state + jnp.dot(activated, down_weight, preferred_element_type=jnp.float32))
        * usable
    ).astype(jnp.bfloat16)
    back_out = (cotangent[0].astype(jnp.float32) * usable).astype(jnp.bfloat16)
    down_full = jnp.einsum("rf,rd->fd", activated, back_out, preferred_element_type=jnp.float32)
    back_act = jnp.einsum("rd,fd->rf", back_out, down_weight, preferred_element_type=jnp.float32)
    back_gate = back_act * up_part * sigmoid_gate * (1.0 + gate_part * (1.0 - sigmoid_gate))
    back_up = back_act * silu_gate
    back_gu = jnp.concatenate([back_gate, back_up], axis=1).astype(jnp.bfloat16)
    gate_up_full = jnp.einsum(
        "rd,rf->df", normed_second, back_gu, preferred_element_type=jnp.float32
    )
    back_second = jnp.einsum(
        "rf,df->rd", back_gu, gate_up_weight, preferred_element_type=jnp.float32
    )
    norm_back, gain_second_grad = rms_back(hidden_state, scale_second, gains_master[1], back_second)
    back_hidden = back_out.astype(jnp.float32) + norm_back
    back_hidden_low = back_hidden.astype(jnp.bfloat16)
    out_full = jnp.einsum(
        "ra,rd->ad", attended, back_hidden_low, preferred_element_type=jnp.float32
    )
    back_attended = jnp.einsum(
        "rd,ad->ra", back_hidden_low, out_weight, preferred_element_type=jnp.float32
    ).astype(jnp.bfloat16)
    back_blocks = back_attended.reshape(local_blocks, BLOCK, KV_HEADS, grouped, HEAD)
    query_grads = []
    key_grads = []
    value_grads = []
    for group_index in range(KV_HEADS):
        query_group = query_blocks[:, :, group_index]
        key_group = window_rows[:, :, group_index * HEAD : (group_index + 1) * HEAD]
        value_group = window_rows[
            :, :, width_kv + group_index * HEAD : width_kv + (group_index + 1) * HEAD
        ]
        scores = scores_for(query_group, key_group, allowed)
        weights_full = jnp.exp(scores - lse_parts[group_index])
        weights_low = weights_full.astype(jnp.bfloat16)
        upstream = back_blocks[:, :, group_index]
        back_weights = jnp.einsum(
            "nqrd,nkd->nrqk", upstream, value_group, preferred_element_type=jnp.float32
        )
        delta = jnp.sum(weights_full * back_weights, axis=-1, keepdims=True)
        back_scores = (weights_full * (back_weights - delta)).astype(jnp.bfloat16)
        query_grads.append(
            jnp.einsum("nrqk,nkd->nqrd", back_scores, key_group, preferred_element_type=jnp.float32)
            * 0.125
        )
        key_grads.append(
            jnp.einsum(
                "nrqk,nqrd->nkd", back_scores, query_group, preferred_element_type=jnp.float32
            )
            * 0.125
        )
        value_grads.append(
            jnp.einsum("nrqk,nqrd->nkd", weights_low, upstream, preferred_element_type=jnp.float32)
        )
    back_window = jnp.concatenate(key_grads + value_grads, axis=-1)
    back_slots = (
        jnp.zeros((blocks_total, BLOCK, 2 * width_kv), jnp.float32)
        .at[key_slots.reshape(-1)]
        .add(back_window.reshape(local_blocks * window, BLOCK, 2 * width_kv))
    )
    back_own = lax.psum_scatter(
        back_slots.reshape(blocks_total * BLOCK, 2 * width_kv),
        "dp",
        scatter_dimension=0,
        tiled=True,
    )
    query_back = unrotate(
        jnp.stack(query_grads, axis=2).reshape(rows_local, HEADS, HEAD), cosine_table, sine_table
    )
    key_back = unrotate(
        back_own[:, :width_kv].reshape(rows_local, KV_HEADS, HEAD), cosine_table, sine_table
    )
    back_proj = jnp.concatenate(
        [
            query_back.reshape(rows_local, width_q),
            key_back.reshape(rows_local, width_kv),
            back_own[:, width_kv:],
        ],
        axis=1,
    ).astype(jnp.bfloat16)
    qkv_full = jnp.einsum("rd,rc->dc", normed_first, back_proj, preferred_element_type=jnp.float32)
    back_first = jnp.einsum("rc,dc->rd", back_proj, qkv_weight, preferred_element_type=jnp.float32)
    input_back, gain_first_grad = rms_back(source, scale_first, gains_master[0], back_first)
    input_grad = (back_hidden + input_back).astype(jnp.bfloat16)
    gains_local = jnp.stack([gain_first_grad, gain_second_grad])
    part_qkv, part_out, part_gate_up, part_down, part_gains = (
        lax.psum_scatter(qkv_full, "dp", scatter_dimension=1, tiled=True),
        lax.psum_scatter(out_full, "dp", scatter_dimension=1, tiled=True),
        lax.psum_scatter(gate_up_full, "dp", scatter_dimension=1, tiled=True),
        lax.psum_scatter(down_full, "dp", scatter_dimension=1, tiled=True),
        lax.psum_scatter(
            jnp.tile(gains_local, (1, data_count)), "dp", scatter_dimension=1, tiled=True
        ),
    )
    qkv_grad, out_grad, gate_up_grad, down_grad, gains_grad = (
        lax.psum_scatter(part_qkv, "shard", scatter_dimension=0, tiled=True),
        lax.psum_scatter(part_out, "shard", scatter_dimension=0, tiled=True),
        lax.psum_scatter(part_gate_up, "shard", scatter_dimension=0, tiled=True),
        lax.psum_scatter(part_down, "shard", scatter_dimension=0, tiled=True),
        lax.psum_scatter(
            jnp.tile(part_gains, (1, owner_count)), "shard", scatter_dimension=1, tiled=True
        ),
    )
    qkv_all = adamw(qkv_master, qkv_grad, qkv_first, qkv_second, MATRIX_RATE, WEIGHT_DECAY)
    out_all = adamw(out_master, out_grad, out_first, out_second, MATRIX_RATE, WEIGHT_DECAY)
    gate_up_all = adamw(
        gate_up_master, gate_up_grad, gate_up_first, gate_up_second, MATRIX_RATE, WEIGHT_DECAY
    )
    down_all = adamw(down_master, down_grad, down_first, down_second, MATRIX_RATE, WEIGHT_DECAY)
    gains_all = adamw(gains_master, gains_grad, gains_first, gains_second, GAIN_RATE, 0.0)
    return (
        layer_out[None],
        input_grad[None],
        qkv_all[0],
        qkv_all[1],
        qkv_all[2],
        qkv_all[3],
        out_all[0],
        out_all[1],
        out_all[2],
        out_all[3],
        gate_up_all[0],
        gate_up_all[1],
        gate_up_all[2],
        gate_up_all[3],
        down_all[0],
        down_all[1],
        down_all[2],
        down_all[3],
        gains_all[0],
        gains_all[1],
        gains_all[2],
        gains_all[3],
    )


def solution(mesh):
    in_specs = (
        P("shard", "dp", None),
        P("shard", "dp", None),
        P("shard", None),
        P("shard", None),
        P("shard", "dp"),
        P("shard", "dp"),
        P("shard", "dp"),
        P("shard", "dp"),
        P("shard", "dp"),
        P("shard", "dp"),
        P("shard", "dp"),
        P("shard", "dp"),
        P("shard", "dp"),
        P("shard", "dp"),
        P("shard", "dp"),
        P("shard", "dp"),
        P(),
        P(),
        P(),
    )
    out_specs = (
        P("shard", "dp", None),
        P("shard", "dp", None),
        P("shard", "dp"),
        P("shard", "dp"),
        P("shard", "dp"),
        P("shard", "dp"),
        P("shard", "dp"),
        P("shard", "dp"),
        P("shard", "dp"),
        P("shard", "dp"),
        P("shard", "dp"),
        P("shard", "dp"),
        P("shard", "dp"),
        P("shard", "dp"),
        P("shard", "dp"),
        P("shard", "dp"),
        P("shard", "dp"),
        P("shard", "dp"),
        P(),
        P(),
        P(),
        P(),
    )
    return jax.shard_map(body, mesh=mesh, in_specs=in_specs, out_specs=out_specs, check_vma=False)
```

profile of v0, /device:TPU:0, one launch (start us, length us, event | category | flops | bytes accessed | tf_op | source)
XLA Modules:
  0.0 1407.2 jit_solution(12777098826401581552)
XLA Ops:
  8.2 33.9 %all_gather.27 = bf16[240,1600]{0,1:T(8,128)(2,1)S(1)} all-gather(bf16[240,200]{0,1:T(8,128)(2,1)S(1)} %convert_element_type.144), channel_id=1, replica_groups=mesh['dp'=8,'shard'=4] {'dp'}, dimensions={1}, use_global_device_ids=true | all-gather | bytes 864000 | tf_op jit(solution)/shard_map/all_gather | solution.py:135
  49.1 24.3 %all-gather.8.cloned.1.call-done = bf16[960,1600]{1,0:T(8,128)(2,1)} async-done(((bf16[240,1600]{1,0:T(8,128)(2,1)}), bf16[960,1600]{1,0:T(8,128)(2,1)}) %all-gather.8.cloned.1.call-update) | async-done | bytes 3072016 | tf_op jit(solution)/shard_map/all_gather | solution.py:141
  77.9 32.3 %all_gather.30 = bf16[240,960]{0,1:T(8,128)(2,1)S(1)} all-gather(bf16[240,120]{0,1:T(8,128)(2,1)S(1)} %copy.159), channel_id=1, replica_groups=mesh['dp'=8,'shard'=4] {'dp'}, dimensions={1}, use_global_device_ids=true | all-gather | bytes 518400 | tf_op jit(solution)/shard_map/all_gather | solution.py:136
  111.3 19.1 %all-gather.14.cloned.1.call-done = bf16[240,5120]{1,0:T(8,128)(2,1)} async-done(((bf16[240,640]{1,0:T(8,128)(2,1)}), bf16[240,5120]{1,0:T(8,128)(2,1)}) %all-gather.14.cloned.1.call-update) | async-done | bytes 2457616 | tf_op jit(solution)/shard_map/all_gather | solution.py:137
  133.5 40.5 %all-gather.18.cloned.1.call-done = bf16[640,960]{0,1:T(8,128)(2,1)} async-done(((bf16[640,120]{0,1:T(8,128)(2,1)}), bf16[640,960]{0,1:T(8,128)(2,1)}) %all-gather.18.cloned.1.call-update) | async-done | bytes 1228816 | tf_op jit(solution)/shard_map/all_gather | solution.py:138
  175.2 42.4 %all-gather.10.cloned.1.call-done = bf16[1024,640]{0,1:T(8,128)(2,1)} async-done(((bf16[128,640]{0,1:T(8,128)(2,1)}), bf16[1024,640]{0,1:T(8,128)(2,1)}) %all-gather.10.cloned.1.call-update) | async-done | bytes 1310736 | tf_op jit(solution)/shard_map/all_gather | solution.py:194
  224.4 15.7 %all-gather.12.cloned.1.call-done = bf16[960,960]{1,0:T(8,128)(2,1)} async-done(((bf16[240,960]{1,0:T(8,128)(2,1)}), bf16[960,960]{1,0:T(8,128)(2,1)}) %all-gather.12.cloned.1.call-update) | async-done | bytes 1843216 | tf_op jit(solution)/shard_map/all_gather | solution.py:142
  243.6 64.5 %all-gather.16.cloned.1.call-done = bf16[960,5120]{1,0:T(8,128)(2,1)} async-done(((bf16[240,5120]{1,0:T(8,128)(2,1)}), bf16[960,5120]{1,0:T(8,128)(2,1)}) %all-gather.16.cloned.1.call-update) | async-done | bytes 9830416 | tf_op jit(solution)/shard_map/all_gather | solution.py:143
  308.1 6.9 fusion.159
  315.0 33.2 %all-gather.20.cloned.1.call-done = bf16[2560,960]{0,1:T(8,128)(2,1)} async-done(((bf16[640,960]{0,1:T(8,128)(2,1)}), bf16[2560,960]{0,1:T(8,128)(2,1)}) %all-gather.20.cloned.1.call-update) | async-done | bytes 4915216 | tf_op jit(solution)/shard_map/all_gather | solution.py:144
  348.2 5.6 multiply_convert_fusion.1
  378.4 64.7 %reduce-scatter.20.cloned.1.call-done = f32[128,640]{1,0:T(8,128)} async-done(((f32[1024,640]{1,0:T(8,128)}), f32[128,640]{1,0:T(8,128)}) %reduce-scatter.20.cloned.1.call-update) | async-done | bytes 327696 | tf_op jit(solution)/shard_map/reduce_scatter | solution.py:293
  460.0 5.2 fusion.86
  466.5 8.3 fusion.49
  474.9 59.9 %reduce-scatter.38.cloned.1.call-done = f32[960,2]{1,0:T(8,128)} async-done(((f32[7680,2]{1,0:T(8,128)}), f32[960,2]{1,0:T(8,128)}) %reduce-scatter.38.cloned.1.call-update) | async-done | bytes 7696
  537.3 85.5 %reduce-scatter.36.cloned.1.call-done = f32[120,960]{1,0:T(8,128)} async-done(((f32[960,960]{1,0:T(8,128)}), f32[120,960]{1,0:T(8,128)}) %reduce-scatter.36.cloned.1.call-update) | async-done | bytes 460816
  624.8 122.9 %reduce-scatter.22.cloned.1.call-done = f32[960,200]{0,1:T(8,128)} async-done(((f32[960,1600]{0,1:T(8,128)}), f32[960,200]{0,1:T(8,128)}) %reduce-scatter.22.cloned.1.call-update) | async-done | bytes 768016 | tf_op jit(solution)/shard_map/reduce_scatter | solution.py:319
  750.3 169.6 %reduce-scatter.30.cloned.1.call-done = f32[2560,120]{0,1:T(8,128)} async-done(((f32[2560,960]{0,1:T(8,128)}), f32[2560,120]{0,1:T(8,128)}) %reduce-scatter.30.cloned.1.call-update) | async-done | bytes 1228816 | tf_op jit(solution)/shard_map/reduce_scatter | solution.py:322
  920.2 327.3 %reduce-scatter.26.cloned.1.call-done = f32[960,640]{1,0:T(8,128)} async-done(((f32[960,5120]{1,0:T(8,128)}), f32[960,640]{1,0:T(8,128)}) %reduce-scatter.26.cloned.1.call-update) | async-done | bytes 2457616 | tf_op jit(solution)/shard_map/reduce_scatter | solution.py:321
  1253.1 26.8 %reduce-scatter.40.cloned.1.call-done = f32[960,2]{1,0:T(8,128)} async-done(((f32[3840,2]{1,0:T(8,128)}), f32[960,2]{1,0:T(8,128)}) %reduce-scatter.40.cloned.1.call-update) | async-done | bytes 7696
  1281.8 23.1 %reduce-scatter.24.cloned.1.call-done = f32[240,120]{1,0:T(8,128)} async-done(((f32[960,120]{1,0:T(8,128)}), f32[240,120]{1,0:T(8,128)}) %reduce-scatter.24.cloned.1.call-update) | async-done | bytes 115216 | tf_op jit(solution)/shard_map/reduce_scatter | solution.py:329
  1306.5 25.3 %reduce-scatter.34.cloned.1.call-done = f32[240,200]{1,0:T(8,128)} async-done(((f32[960,200]{1,0:T(8,128)}), f32[240,200]{1,0:T(8,128)}) %reduce-scatter.34.cloned.1.call-update) | async-done | bytes 192016
  1333.8 27.2 %reduce-scatter.32.cloned.1.call-done = f32[640,120]{0,1:T(8,128)} async-done(((f32[2560,120]{0,1:T(8,128)}), f32[640,120]{0,1:T(8,128)}) %reduce-scatter.32.cloned.1.call-update) | async-done | bytes 307216 | tf_op jit(solution)/shard_map/reduce_scatter | solution.py:331
  1363.1 34.6 %reduce-scatter.28.cloned.1.call-done = f32[240,640]{1,0:T(8,128)} async-done(((f32[960,640]{1,0:T(8,128)}), f32[240,640]{1,0:T(8,128)}) %reduce-scatter.28.cloned.1.call-update) | async-done | bytes 614416 | tf_op jit(solution)/shard_map/reduce_scatter | solution.py:330
  (337 shorter events, 89.7 us)
Async XLA Ops:
  7.2 66.2 %all-gather.8.cloned.1.call-start = ((), (), s32[]{:S(2)}) async-start(), calls=%async_computation.11 | async-start | bytes 3993600 | tf_op jit(solution)/shard_map/all_gather | solution.py:141
  43.5 86.9 %all-gather.14.cloned.1.call-start = ((), (), s32[]{:S(2)}) async-start(), calls=%async_computation.14 | async-start | bytes 2764800 | tf_op jit(solution)/shard_map/all_gather | solution.py:137
  44.3 129.7 %all-gather.18.cloned.1.call-start = ((), (), s32[]{:S(2)}) async-start(), calls=%async_computation.16 | async-start | bytes 1382400 | tf_op jit(solution)/shard_map/all_gather | solution.py:138
  45.1 172.4 %all-gather.10.cloned.1.call-start = ((), (), s32[]{:S(2)}) async-start(), calls=%async_computation.12 | async-start | bytes 1474560 | tf_op jit(solution)/shard_map/all_gather | solution.py:194
  49.1 126.0 %copy-start.39 = (f32[128,32]{0,1:T(8,128)}, f32[128,32]{0,1:T(8,128)S(1)}, u32[]{:S(2)}) copy-start(f32[128,32]{0,1:T(8,128)S(1)} %get-tuple-element.92) | copy-start | bytes 49156
  77.7 162.4 %all-gather.12.cloned.1.call-start = ((), (), s32[]{:S(2)}) async-start(), calls=%async_computation.13 | async-start | bytes 2457600 | tf_op jit(solution)/shard_map/all_gather | solution.py:142
  111.2 196.8 %all-gather.16.cloned.1.call-start = ((), (), s32[]{:S(2)}) async-start(), calls=%async_computation.15 | async-start | bytes 12288000 | tf_op jit(solution)/shard_map/all_gather | solution.py:143
  130.3 217.8 %all-gather.20.cloned.1.call-start = ((), (), s32[]{:S(2)}) async-start(), calls=%async_computation.17 | async-start | bytes 6144000 | tf_op jit(solution)/shard_map/all_gather | solution.py:144
  174.0 269.0 %reduce-scatter.20.cloned.1.call-start = ((), (), s32[]{:S(2)}) async-start(), calls=%async_computation.18 | async-start | bytes 2949120 | tf_op jit(solution)/shard_map/reduce_scatter | solution.py:293
  242.9 116.0 %copy-start.53 = (f32[3,128]{1,0:T(4,128)}, f32[3,128]{1,0:T(4,128)S(1)}, u32[]{:S(2)}) copy-start(f32[3,128]{1,0:T(4,128)S(1)} %log_add_fusion) | copy-start | bytes 4612
  372.3 162.5 %reduce-scatter.38.cloned.1.call-start = ((), (), s32[]{:S(2)}) async-start(), calls=%async_computation.27 | async-start | bytes 4423680
  451.4 171.3 %reduce-scatter.36.cloned.1.call-start = ((), (), s32[]{:S(2)}) async-start(), calls=%async_computation.26 | async-start | bytes 4423680
  455.0 292.8 %reduce-scatter.22.cloned.1.call-start = ((), (), s32[]{:S(2)}) async-start(), calls=%async_computation.19 | async-start | bytes 7372800 | tf_op jit(solution)/shard_map/reduce_scatter | solution.py:319
  458.9 461.0 %reduce-scatter.30.cloned.1.call-start = ((), (), s32[]{:S(2)}) async-start(), calls=%async_computation.23 | async-start | bytes 11059200 | tf_op jit(solution)/shard_map/reduce_scatter | solution.py:322
  465.2 782.2 %reduce-scatter.26.cloned.1.call-start = ((), (), s32[]{:S(2)}) async-start(), calls=%async_computation.21 | async-start | bytes 22118400 | tf_op jit(solution)/shard_map/reduce_scatter | solution.py:321
  474.8 805.1 %reduce-scatter.40.cloned.1.call-start = ((), (), s32[]{:S(2)}) async-start(), calls=%async_computation.28 | async-start | bytes 2457600
  537.2 767.6 %reduce-scatter.24.cloned.1.call-start = ((), (), s32[]{:S(2)}) async-start(), calls=%async_computation.20 | async-start | bytes 614400 | tf_op jit(solution)/shard_map/reduce_scatter | solution.py:329
  624.8 707.0 %reduce-scatter.34.cloned.1.call-start = ((), (), s32[]{:S(2)}) async-start(), calls=%async_computation.25 | async-start | bytes 1228800
  750.2 610.8 %reduce-scatter.32.cloned.1.call-start = ((), (), s32[]{:S(2)}) async-start(), calls=%async_computation.24 | async-start | bytes 1536000 | tf_op jit(solution)/shard_map/reduce_scatter | solution.py:331
  919.9 477.9 %reduce-scatter.28.cloned.1.call-start = ((), (), s32[]{:S(2)}) async-start(), calls=%async_computation.22 | async-start | bytes 3072000 | tf_op jit(solution)/shard_map/reduce_scatter | solution.py:330
  1252.2 80.7 %copy-start.30 = (f32[240,200]{0,1:T(8,128)S(1)}, f32[240,200]{0,1:T(8,128)}, u32[]{:S(2)}) copy-start(f32[240,200]{0,1:T(8,128)} %param.25) | copy-start | bytes 576004
  1252.2 80.7 %copy-start.43 = (f32[240,200]{0,1:T(8,128)S(1)}, f32[240,200]{0,1:T(8,128)}, u32[]{:S(2)}) copy-start(f32[240,200]{0,1:T(8,128)} %param.27) | copy-start | bytes 576004
  1252.2 80.7 %copy-start.44 = (f32[240,200]{0,1:T(8,128)S(1)}, f32[240,200]{0,1:T(8,128)}, u32[]{:S(2)}) copy-start(f32[240,200]{0,1:T(8,128)} %param.26) | copy-start | bytes 576004
  1281.7 79.3 %copy-start.42 = (f32[640,120]{0,1:T(8,128)S(1)}, f32[640,120]{0,1:T(8,128)}, u32[]{:S(2)}) copy-start(f32[640,120]{0,1:T(8,128)} %param.35) | copy-start | bytes 921604
  (76 other events, 966.5 us)
Sparse Core Ops, SparseCore 0:
  43.6 29.7 all-gather.7
  76.2 54.0 all-gather.13
  133.1 40.8 all-gather.17
  176.4 41.0 all-gather.9
  219.5 20.5 all-gather.11
  241.5 66.4 all-gather.15
  309.6 38.5 all-gather.19
  372.4 70.6 reduce-scatter.19
  451.5 83.1 reduce-scatter.37
  538.7 83.9 reduce-scatter.35
  626.4 121.3 reduce-scatter.21
  751.7 168.0 reduce-scatter.29
  924.3 323.1 reduce-scatter.25
  1250.0 29.7 reduce-scatter.39
  1283.4 21.4 reduce-scatter.23
  1307.3 24.4 reduce-scatter.33
  1335.0 26.0 reduce-scatter.31
  1364.1 33.6 reduce-scatter.27
where the time goes:
time: 1410 us
  waiting for transfers between devices  1210 us (86%)
  blocking collectives  66.2 us (5%)
  matrix products  63.5 us (5%)
  local copies, waits for them, and re-layouts  29.6 us (2%)
  other arithmetic  21.4 us (2%)
  between operations  18.9 us (1%)
    reduce_scatter x1, waiting for transfers between devices, body(): lax.psum_scatter(gate_up_full, 'dp', scatter_dimension=1, tiled=True)  327 us
    unnamed x22, waiting for transfers between devices  198 us
    reduce_scatter x1, waiting for transfers between devices, body(): lax.psum_scatter(down_full, 'dp', scatter_dimension=1, tiled=True)  170 us
    reduce_scatter x1, waiting for transfers between devices, body(): lax.psum_scatter(qkv_full, 'dp', scatter_dimension=1, tiled=True)  123 us
    reduce_scatter x1, waiting for transfers between devices, body(): lax.psum_scatter(back_slots.reshape(blocks_total * BLOCK, 2 * width_kv),...  64.7 us
    all_gather x1, waiting for transfers between devices, body(): lax.all_gather(gate_up_cols, 'shard', axis=0, tiled=True)  64.5 us
    all_gather x1, waiting for transfers between devices, body(): gathered = lax.all_gather(keys_values, 'dp', axis=0, tiled=True)  42.4 us
    all_gather x1, waiting for transfers between devices, body(): lax.all_gather(down_low, 'dp', axis=1, tiled=True)  40.5 us
  transfers between devices with their start and end apart: 18, of which 18 were waited for; matrix products, arithmetic and copies ran while one was open for 5% of the time, Pallas kernels for 0%

commit v1 on v0

--- a/solution.py
+++ b/solution.py
@@ -1,8 +1,11 @@
+import functools
 import math
 
 import jax
 import jax.numpy as jnp
 from jax import lax
+from jax.experimental import pallas as pl
+from jax.experimental.pallas import tpu as pltpu
 from jax.sharding import PartitionSpec as P
 
 HEADS = 15
@@ -93,6 +96,121 @@
     second_new = 0.95 * second + 0.05 * grad * grad
     update = first_new / (1.0 - 0.9**STEP) / (jnp.sqrt(second_new / (1.0 - 0.95**STEP)) + 1e-08)
     return (grad, first_new, second_new, master - rate * (update + decay * master))
+
+MESH = pl.DeviceIdType.MESH
+LOW = jnp.bfloat16
+
+
+def exchange_kernel(count, axis, whole, *refs):
+    number = len(whole)
+    sources, targets = refs[:number], refs[number : 2 * number]
+    send_sems, recv_sems, local_sems = refs[2 * number :]
+    me = lax.axis_index(axis)
+    barrier = pltpu.get_barrier_semaphore()
+    for step in range(1, count):
+        pl.semaphore_signal(
+            barrier,
+            inc=1,
+            device_id={axis: lax.rem(me + step, count)},
+            device_id_type=MESH,
+        )
+    pl.semaphore_wait(barrier, count - 1)
+    copies = []
+    for step in range(1, count):
+        peer = lax.rem(me + step, count)
+        for index in range(number):
+            copy = pltpu.make_async_remote_copy(
+                src_ref=sources[index] if whole[index] else sources[index].at[peer],
+                dst_ref=targets[index].at[me],
+                send_sem=send_sems.at[index, step - 1],
+                recv_sem=recv_sems.at[index, step - 1],
+                device_id={axis: peer},
+                device_id_type=MESH,
+            )
+            copy.start()
+            copies.append(copy)
+    locals_ = []
+    for index in range(number):
+        copy = pltpu.make_async_copy(
+            sources[index] if whole[index] else sources[index].at[me],
+            targets[index].at[me],
+            local_sems.at[index],
+        )
+        copy.start()
+        locals_.append(copy)
+    for copy in locals_:
+        copy.wait()
+    for copy in copies:
+        copy.wait()
+
+
+def exchange(ident, axis, whole, *arrays):
+    count = lax.axis_size(axis)
+    if any(array.shape[-2] % 16 for array in arrays):
+        return [
+            lax.all_gather(array, axis) if all_of_it else lax.all_to_all(array, axis, 0, 0)
+            for array, all_of_it in zip(arrays, whole)
+        ]
+    shapes = [
+        jax.ShapeDtypeStruct((count,) + array.shape[-2:], array.dtype) for array in arrays
+    ]
+    number = len(arrays)
+    return pl.pallas_call(
+        functools.partial(exchange_kernel, count, axis, tuple(whole)),
+        out_shape=shapes,
+        in_specs=[pl.BlockSpec(memory_space=pl.ANY)] * number,
+        out_specs=[pl.BlockSpec(memory_space=pl.ANY)] * number,
+        scratch_shapes=[
+            pltpu.SemaphoreType.DMA((number, count - 1)),
+            pltpu.SemaphoreType.DMA((number, count - 1)),
+            pltpu.SemaphoreType.DMA((number,)),
+        ],
+        compiler_params=pltpu.CompilerParams(collective_id=ident, has_side_effects=True),
+    )(*arrays)
+
+
+def shared(ident, *arrays):
+    return exchange(ident, "shard", [True] * len(arrays), *arrays)
+
+
+def dealt(ident, *arrays):
+    return exchange(ident, "shard", [False] * len(arrays), *arrays)
+
+
+def to_pieces(array, count):
+    rows, columns = array.shape
+    return array.reshape(rows, count, columns // count).transpose(1, 0, 2)
+
+
+def from_pieces(array):
+    count, rows, columns = array.shape
+    return array.transpose(1, 0, 2).reshape(rows, count * columns)
+
+
+def added(array):
+    return jnp.sum(array.astype(jnp.float32), axis=0)
+
+
+def nt(left, right):
+    return lax.dot_general(
+        left, right, (((1,), (1,)), ((), ())), preferred_element_type=jnp.float32
+    )
+
+
+def nn(left, right):
+    return jnp.dot(left, right, preferred_element_type=jnp.float32)
+
+
+def tn(left, right):
+    return lax.dot_general(
+        left, right, (((0,), (0,)), ((), ())), preferred_element_type=jnp.float32
+    )
+
+
+def data_sum(array):
+    return lax.psum_scatter(
+        array.astype(LOW), "dp", scatter_dimension=0, tiled=True
+    ).astype(jnp.float32)
 
 
 def body(
@@ -125,24 +243,24 @@
     grouped = HEADS // KV_HEADS
     width_q = HEADS * HEAD
     width_kv = KV_HEADS * HEAD
-    data_count = lax.axis_size("dp")
     owner_count = lax.axis_size("shard")
-    qkv_low = qkv_master.astype(jnp.bfloat16)
-    out_low = out_master.astype(jnp.bfloat16)
-    gate_up_low = gate_up_master.astype(jnp.bfloat16)
-    down_low = down_master.astype(jnp.bfloat16)
-    qkv_cols, out_cols, gate_up_cols, down_cols = (
-        lax.all_gather(qkv_low, "dp", axis=1, tiled=True),
-        lax.all_gather(out_low, "dp", axis=1, tiled=True),
-        lax.all_gather(gate_up_low, "dp", axis=1, tiled=True),
-        lax.all_gather(down_low, "dp", axis=1, tiled=True),
-    )
-    qkv_weight, out_weight, gate_up_weight, down_weight = (
-        lax.all_gather(qkv_cols, "shard", axis=0, tiled=True),
-        lax.all_gather(out_cols, "shard", axis=0, tiled=True),
-        lax.all_gather(gate_up_cols, "shard", axis=0, tiled=True),
-        lax.all_gather(down_cols, "shard", axis=0, tiled=True),
-    )
+    chunk = gate_up_master.shape[1] // owner_count
+    span = down_master.shape[0] // (owner_count * chunk)
+    qkv_t = lax.all_gather(qkv_master.T.astype(LOW), "dp", axis=0, tiled=True)
+    out_t = lax.all_gather(out_master.T.astype(LOW), "dp", axis=0, tiled=True)
+    gate_up_dealt, down_dealt = dealt(
+        0,
+        gate_up_master.T.astype(LOW).reshape(owner_count, chunk, -1),
+        down_master.astype(LOW)
+        .reshape(span, owner_count, chunk, -1)
+        .transpose(1, 0, 2, 3)
+        .reshape(owner_count, span * chunk, -1),
+    )
+    gate_up_t = lax.all_gather(from_pieces(gate_up_dealt), "dp", axis=0, tiled=True)
+    down_t = lax.all_gather(
+        down_dealt.reshape(owner_count * span * chunk, -1).T, "dp", axis=0, tiled=True
+    )
+    every = owner_count * rows_local
     labels_all, position_all, usable_all = layout(lengths, blocks_total)
     slot_index = jnp.arange(blocks_total, dtype=jnp.int32)
     local_slots = lax.axis_index("dp") * local_blocks + jnp.arange(local_blocks, dtype=jnp.int32)
@@ -174,10 +292,16 @@
     allowed = (query_labels[:, :, None] == key_labels[:, None, :]) & (
         key_order[:, None, :] <= query_order[:, :, None]
     )
+    back_out = (cotangent[0].astype(jnp.float32) * usable).astype(LOW)
     source = tokens[0].astype(jnp.float32)
     scale_first = lax.rsqrt(jnp.mean(source * source, axis=-1, keepdims=True) + NORM_EPS)
-    normed_first = (source * scale_first * gains_master[0]).astype(jnp.bfloat16)
-    projected = jnp.dot(normed_first, qkv_weight, preferred_element_type=jnp.float32)
+    normed_first = (source * scale_first * gains_master[0]).astype(LOW)
+    (normed_dealt,) = dealt(1, to_pieces(normed_first, owner_count))
+    normed_slab = normed_dealt.reshape(every, -1)
+    (projected_parts,) = dealt(
+        2, nt(normed_slab, qkv_t).astype(LOW).reshape(owner_count, rows_local, -1)
+    )
+    projected = added(projected_parts)
     cosine_table, sine_table = rope_tables(query_position)
     queries = rotate(
         projected[:, :width_q].reshape(rows_local, HEADS, HEAD), cosine_table, sine_table
@@ -216,42 +340,48 @@
         )
         lse_parts.append(top_score + jnp.log(totals))
     attended = jnp.stack(mixed_parts, axis=2).reshape(rows_local, width_q).astype(jnp.bfloat16)
-    hidden_state = source + jnp.dot(attended, out_weight, preferred_element_type=jnp.float32)
+    (attended_dealt,) = dealt(3, to_pieces(attended, owner_count))
+    attended_slab = attended_dealt.reshape(every, -1)
+    (mixed_sums,) = dealt(
+        4, nt(attended_slab, out_t).astype(LOW).reshape(owner_count, rows_local, -1)
+    )
+    hidden_state = source + added(mixed_sums)
     scale_second = lax.rsqrt(
         jnp.mean(hidden_state * hidden_state, axis=-1, keepdims=True) + NORM_EPS
     )
-    normed_second = (hidden_state * scale_second * gains_master[1]).astype(jnp.bfloat16)
-    gate_up = jnp.dot(normed_second, gate_up_weight, preferred_element_type=jnp.float32)
-    gate_part = gate_up[:, :FF]
-    up_part = gate_up[:, FF:]
+    normed_second = (hidden_state * scale_second * gains_master[1]).astype(LOW)
+    normed_all, back_out_all = shared(5, normed_second, back_out)
+    normed_all = normed_all.reshape(every, -1)
+    back_out_all = back_out_all.reshape(every, -1)
+    gate_up = nt(normed_all, gate_up_t)
+    units = gate_up.shape[1] // 2
+    gate_part = gate_up[:, :units]
+    up_part = gate_up[:, units:]
     sigmoid_gate = jax.nn.sigmoid(gate_part)
     silu_gate = gate_part * sigmoid_gate
-    activated = (silu_gate * up_part).astype(jnp.bfloat16)
-    layer_out = (
-        (hidden_state + jnp.dot(activated, down_weight, preferred_element_type=jnp.float32))
-        * usable
-    ).astype(jnp.bfloat16)
-    back_out = (cotangent[0].astype(jnp.float32) * usable).astype(jnp.bfloat16)
-    down_full = jnp.einsum("rf,rd->fd", activated, back_out, preferred_element_type=jnp.float32)
-    back_act = jnp.einsum("rd,fd->rf", back_out, down_weight, preferred_element_type=jnp.float32)
+    activated = (silu_gate * up_part).astype(LOW)
+    back_act = nn(back_out_all, down_t)
     back_gate = back_act * up_part * sigmoid_gate * (1.0 + gate_part * (1.0 - sigmoid_gate))
     back_up = back_act * silu_gate
-    back_gu = jnp.concatenate([back_gate, back_up], axis=1).astype(jnp.bfloat16)
-    gate_up_full = jnp.einsum(
-        "rd,rf->df", normed_second, back_gu, preferred_element_type=jnp.float32
-    )
-    back_second = jnp.einsum(
-        "rf,df->rd", back_gu, gate_up_weight, preferred_element_type=jnp.float32
-    )
+    back_gu = jnp.concatenate([back_gate, back_up], axis=1).astype(LOW)
+    down_parts, second_parts = dealt(
+        6,
+        nt(activated, down_t).astype(LOW).reshape(owner_count, rows_local, -1),
+        nn(back_gu, gate_up_t).astype(LOW).reshape(owner_count, rows_local, -1),
+    )
+    down_sum = data_sum(tn(back_out_all, activated))
+    gate_up_sum = data_sum(tn(back_gu, normed_all))
+    layer_out = ((hidden_state + added(down_parts)) * usable).astype(LOW)
+    back_second = added(second_parts)
     norm_back, gain_second_grad = rms_back(hidden_state, scale_second, gains_master[1], back_second)
     back_hidden = back_out.astype(jnp.float32) + norm_back
-    back_hidden_low = back_hidden.astype(jnp.bfloat16)
-    out_full = jnp.einsum(
-        "ra,rd->ad", attended, back_hidden_low, preferred_element_type=jnp.float32
-    )
-    back_attended = jnp.einsum(
-        "rd,ad->ra", back_hidden_low, out_weight, preferred_element_type=jnp.float32
-    ).astype(jnp.bfloat16)
+    (back_hidden_all,) = shared(7, back_hidden.astype(LOW))
+    back_hidden_all = back_hidden_all.reshape(every, -1)
+    (back_att_pieces,) = dealt(
+        8, nn(back_hidden_all, out_t).astype(LOW).reshape(owner_count, rows_local, -1)
+    )
+    out_sum = data_sum(tn(back_hidden_all, attended_slab))
+    back_attended = from_pieces(back_att_pieces)
     back_blocks = back_attended.reshape(local_blocks, BLOCK, KV_HEADS, grouped, HEAD)
     query_grads = []
     key_grads = []
@@ -290,12 +420,7 @@
         .at[key_slots.reshape(-1)]
         .add(back_window.reshape(local_blocks * window, BLOCK, 2 * width_kv))
     )
-    back_own = lax.psum_scatter(
-        back_slots.reshape(blocks_total * BLOCK, 2 * width_kv),
-        "dp",
-        scatter_dimension=0,
-        tiled=True,
-    )
+    back_own = data_sum(back_slots.reshape(blocks_total * BLOCK, 2 * width_kv))
     query_back = unrotate(
         jnp.stack(query_grads, axis=2).reshape(rows_local, HEADS, HEAD), cosine_table, sine_table
     )
@@ -310,29 +435,27 @@
         ],
         axis=1,
     ).astype(jnp.bfloat16)
-    qkv_full = jnp.einsum("rd,rc->dc", normed_first, back_proj, preferred_element_type=jnp.float32)
-    back_first = jnp.einsum("rc,dc->rd", back_proj, qkv_weight, preferred_element_type=jnp.float32)
+    (back_proj_all,) = shared(9, back_proj)
+    back_proj_all = back_proj_all.reshape(every, -1)
+    gate_up_back, down_back, first_pieces = dealt(
+        10,
+        to_pieces(gate_up_sum.astype(LOW), owner_count),
+        down_sum.T.astype(LOW).reshape(owner_count, span * chunk, -1),
+        nn(back_proj_all, qkv_t).astype(LOW).reshape(owner_count, rows_local, -1),
+    )
+    qkv_grad = data_sum(tn(back_proj_all, normed_slab)).T
+    out_grad = out_sum.T
+    gate_up_grad = gate_up_back.reshape(owner_count * chunk, -1).T.astype(jnp.float32)
+    down_grad = (
+        down_back.reshape(owner_count, span, chunk, -1)
+        .transpose(1, 0, 2, 3)
+        .reshape(down_master.shape)
+        .astype(jnp.float32)
+    )
+    back_first = from_pieces(first_pieces).astype(jnp.float32)
     input_back, gain_first_grad = rms_back(source, scale_first, gains_master[0], back_first)
-    input_grad = (back_hidden + input_back).astype(jnp.bfloat16)
-    gains_local = jnp.stack([gain_first_grad, gain_second_grad])
-    part_qkv, part_out, part_gate_up, part_down, part_gains = (
-        lax.psum_scatter(qkv_full, "dp", scatter_dimension=1, tiled=True),
-        lax.psum_scatter(out_full, "dp", scatter_dimension=1, tiled=True),
-        lax.psum_scatter(gate_up_full, "dp", scatter_dimension=1, tiled=True),
-        lax.psum_scatter(down_full, "dp", scatter_dimension=1, tiled=True),
-        lax.psum_scatter(
-            jnp.tile(gains_local, (1, data_count)), "dp", scatter_dimension=1, tiled=True
-        ),
-    )
-    qkv_grad, out_grad, gate_up_grad, down_grad, gains_grad = (
-        lax.psum_scatter(part_qkv, "shard", scatter_dimension=0, tiled=True),
-        lax.psum_scatter(part_out, "shard", scatter_dimension=0, tiled=True),
-        lax.psum_scatter(part_gate_up, "shard", scatter_dimension=0, tiled=True),
-        lax.psum_scatter(part_down, "shard", scatter_dimension=0, tiled=True),
-        lax.psum_scatter(
-            jnp.tile(part_gains, (1, owner_count)), "shard", scatter_dimension=1, tiled=True
-        ),
-    )
+    input_grad = (back_hidden + input_back).astype(LOW)
+    gains_grad = lax.psum(jnp.stack([gain_first_grad, gain_second_grad]), ("dp", "shard"))
     qkv_all = adamw(qkv_master, qkv_grad, qkv_first, qkv_second, MATRIX_RATE, WEIGHT_DECAY)
     out_all = adamw(out_master, out_grad, out_first, out_second, MATRIX_RATE, WEIGHT_DECAY)
     gate_up_all = adamw(

time: 1410 us -> 714 us (0.51)
  waiting for transfers between devices: 1210 us -> 303 us
  Pallas kernels: 0 us -> 156 us
  blocking collectives: 66.2 us -> 103 us
  local copies, waits for them, and re-layouts: 29.6 us -> 50.8 us
  matrix products: 63.5 us -> 47.6 us
    reduce_scatter x7 -> x4, waiting for transfers between devices: 769 us -> 211 us  [data_sum(): lax.psum_scatter(array.astype(LOW), 'dp', scatter_dimension=0, tiled=True)]
    all_gather x6 -> x2, waiting for transfers between devices: 197 us -> 30.8 us  [the longest x1 30.8 us: body(): lax.all_gather(down_dealt.reshape(owner_count * span * chunk, -1).T, 'dp'...]
    pallas_call x0 -> x11, Pallas kernels: none -> 156 us  [exchange(): pl.pallas_call(functools.partial(exchange_kernel, count, axis, tuple(whol...]
    unnamed x22 -> x9, waiting for transfers between devices: 198 us -> 60.9 us
    all_gather x1, waiting for transfers between devices: 42.4 us -> 0.02 us  [body(): gathered = lax.all_gather(keys_values, 'dp', axis=0, tiled=True)]
    psum x0 -> x1, blocking collectives: none -> 39 us  [body(): lax.psum(jnp.stack([gain_first_grad, gain_second_grad]), ('dp', 'shard'))]
    convert_element_type x0 -> x16, local copies, waits for them, and re-layouts: none -> 20 us  [the longest x1 2.44 us: body(): nt(normed_slab, qkv_t).astype(LOW).reshape(owner_count, rows_local, -1)]
    dot_general x11 -> x12, matrix products: 48.2 us -> 35.2 us  [the longest x4 11.9 us: nn(): return jnp.dot(left, right, preferred_element_type=jnp.float32)]
  transfers between devices with their start and end apart: 18 -> 8, of which waited for: 18 -> 6; matrix products, arithmetic and copies ran while one was open for 5% -> 8% of each run, Pallas kernels for 0% -> 10%
where the time goes in v1:
time: 714 us; the launch traced here: 713 us
  waiting for transfers between devices  303 us (42%)
  Pallas kernels  156 us (22%)
  blocking collectives  103 us (14%)
  local copies, waits for them, and re-layouts  50.8 us (7%)
  matrix products  47.6 us (7%)
  other arithmetic  32.2 us (5%)
  between operations  19.2 us (3%)
    reduce_scatter x4, waiting for transfers between devices, data_sum(): lax.psum_scatter(array.astype(LOW), 'dp', scatter_dimension=0, tiled=True)  211 us
    pallas_call x11, Pallas kernels, exchange(): pl.pallas_call(functools.partial(exchange_kernel, count, axis, tuple(whol...  156 us
    unnamed x9, waiting for transfers between devices  60.9 us
    psum x1, blocking collectives, body(): lax.psum(jnp.stack([gain_first_grad, gain_second_grad]), ('dp', 'shard'))  39 us
    all_gather x1, blocking collectives, body(): qkv_t = lax.all_gather(qkv_master.T.astype(LOW), 'dp', axis=0, tiled=True)  32.9 us
    all_gather x1, blocking collectives, body(): out_t = lax.all_gather(out_master.T.astype(LOW), 'dp', axis=0, tiled=True)  31.6 us
    all_gather x1, waiting for transfers between devices, body(): lax.all_gather(down_dealt.reshape(owner_count * span * chunk, -1).T, 'dp'...  30.8 us
    unnamed x197, local copies, waits for them, and re-layouts  16.2 us
  transfers between devices with their start and end apart: 8, of which 6 were waited for; matrix products, arithmetic and copies ran while one was open for 8% of the time, Pallas kernels for 10%

profile of v1, /device:TPU:0, one launch (start us, length us, event | category | flops | bytes accessed | tf_op | source)
XLA Modules:
  0.0 712.9 jit_solution(3785239317129519539)
XLA Ops:
  11.0 6.7 shard_map.354
  17.7 32.9 %all_gather.15 = bf16[1600,240]{1,0:T(8,128)(2,1)S(1)} all-gather(bf16[200,240]{1,0:T(8,128)(2,1)S(1)} %convert_bitcast_fusion.5), channel_id=1, replica_groups=mesh['dp'=8,'shard'=4] {'dp'}, dimensions={0}, use_global_device_ids=true | all-gather | bytes 864000 | tf_op jit(solution)/shard_map/all_gather | solution.py:249
  54.6 20.7 %shard_map.355 = bf16[4,128,1600]{2,1,0:T(8,128)(2,1)} custom-call(bf16[4,128,1600]{2,1,0:T(8,128)(2,1)} %bitcast.666), custom_call_target="tpu_custom_call" | custom-call | tf_op jit(solution)/shard_map/pallas_call | solution.py:158
  83.4 8.2 %shard_map.359 = (bf16[4,160,240]{2,1,0:T(8,128)(2,1)}, bf16[4,160,120]{2,1,0:T(8,128)(2,1)}) custom-call(bf16[4,160,240]{2,1,0:T(8,128)(2,1)} %bitcast.693, bf16[4,160,120]{2,1,0:T(8,128)(2,1)} %bitcast.706), custom_call_target="tpu_custom_call" | custom-call | tf_op jit(solution)/shard_map/pallas_call | solution.py:158
  99.2 31.6 %all_gather.17 = bf16[960,240]{1,0:T(8,128)(2,1)S(1)} all-gather(bf16[120,240]{1,0:T(8,128)(2,1)S(1)} %convert_bitcast_fusion.6), channel_id=1, replica_groups=mesh['dp'=8,'shard'=4] {'dp'}, dimensions={0}, use_global_device_ids=true | all-gather | bytes 518400 | tf_op jit(solution)/shard_map/all_gather | solution.py:250
  140.7 5.3 shard_map.356
  150.6 13.6 %shard_map.357 = bf16[4,128,960]{2,1,0:T(8,128)(2,1)} custom-call(bf16[4,128,960]{2,1,0:T(8,128)(2,1)} %bitcast.671), custom_call_target="tpu_custom_call" | custom-call | tf_op jit(solution)/shard_map/pallas_call | solution.py:158
  166.7 25.6 %shard_map.358 = (bf16[4,128,960]{2,1,0:T(8,128)(2,1)}, bf16[4,128,960]{2,1,0:T(8,128)(2,1)}) custom-call(bf16[128,960]{1,0:T(8,128)(2,1)} %multiply_convert_fusion.8.refs_0_, bf16[128,960]{1,0:T(8,128)(2,1)} %fusion.60.refs_1_), custom_call_target="tpu_custom_call" | custom-call | tf_op jit(solution)/shard_map/pallas_call | solution.py:158
  192.5 5.2 fusion.156
  197.7 30.8 %all-gather.8.cloned.1.call-done = bf16[960,640]{1,0:T(8,128)(2,1)} async-done(((bf16[120,640]{1,0:T(8,128)(2,1)}), bf16[960,640]{1,0:T(8,128)(2,1)}) %all-gather.8.cloned.1.call-update) | async-done | bytes 1228816 | tf_op jit(solution)/shard_map/all_gather | solution.py:260
  228.5 4.7 multiply_convert_fusion.1
  239.0 3.5 convolution_convert_fusion.4
  244.8 24.9 %shard_map.360 = (bf16[4,128,960]{2,1,0:T(8,128)(2,1)}, bf16[4,128,960]{2,1,0:T(8,128)(2,1)}) custom-call(bf16[4,128,960]{2,1,0:T(8,128)(2,1)} %bitcast.670, bf16[4,128,960]{2,1,0:T(8,128)(2,1)} %bitcast.669), custom_call_target="tpu_custom_call" | custom-call | tf_op jit(solution)/shard_map/pallas_call | solution.py:158
  273.0 14.1 %shard_map.361 = bf16[4,128,960]{2,1,0:T(8,128)(2,1)} custom-call(bf16[128,960]{1,0:T(8,128)(2,1)} %add_convert_fusion.refs_0_), custom_call_target="tpu_custom_call" | custom-call | tf_op jit(solution)/shard_map/pallas_call | solution.py:158
  291.4 5.7 shard_map.362
  324.1 55.6 %reduce-scatter.10.cloned.1.call-done = bf16[128,640]{1,0:T(8,128)(2,1)} async-done(((bf16[1024,640]{1,0:T(8,128)(2,1)}), bf16[128,640]{1,0:T(8,128)(2,1)}) %reduce-scatter.10.cloned.1.call-update) | async-done | bytes 163856 | tf_op jit(solution)/shard_map/reduce_scatter | solution.py:211
  381.9 20.7 %shard_map.363 = bf16[4,128,1600]{2,1,0:T(8,128)(2,1)} custom-call(bf16[128,1600]{1,0:T(8,128)(2,1)} %concatenate.66.refs_0_), custom_call_target="tpu_custom_call" | custom-call | tf_op jit(solution)/shard_map/pallas_call | solution.py:158
  405.8 4.1 convolution_convert_fusion
  412.6 29.3 %reduce-scatter.14.cloned.1.call-done = bf16[120,240]{1,0:T(8,128)(2,1)} async-done(((bf16[960,240]{1,0:T(8,128)(2,1)}), bf16[120,240]{1,0:T(8,128)(2,1)}) %reduce-scatter.14.cloned.1.call-update) | async-done | bytes 57616 | tf_op jit(solution)/shard_map/reduce_scatter | solution.py:211
  445.9 60.7 %reduce-scatter.16.cloned.1.call-done = bf16[120,640]{1,0:T(8,128)(2,1)} async-done(((bf16[960,640]{1,0:T(8,128)(2,1)}), bf16[120,640]{1,0:T(8,128)(2,1)}) %reduce-scatter.16.cloned.1.call-update) | async-done | bytes 153616
  511.4 54.8 %reduce-scatter.12.cloned.1.call-done = bf16[200,240]{1,0:T(8,128)(2,1)} async-done(((bf16[1600,240]{1,0:T(8,128)(2,1)}), bf16[200,240]{1,0:T(8,128)(2,1)}) %reduce-scatter.12.cloned.1.call-update) | async-done | bytes 96016 | tf_op jit(solution)/shard_map/reduce_scatter | solution.py:211
  568.0 71.7 %reduce-scatter.8.cloned.1.call-done = bf16[160,960]{1,0:T(8,128)(2,1)} async-done(((bf16[1280,960]{1,0:T(8,128)(2,1)}), bf16[160,960]{1,0:T(8,128)(2,1)}) %reduce-scatter.8.cloned.1.call-update) | async-done | bytes 307216 | tf_op jit(solution)/shard_map/reduce_scatter | solution.py:211
  641.8 10.6 %shard_map.364 = (bf16[4,160,240]{2,1,0:T(8,128)(2,1)}, bf16[4,160,120]{2,1,0:T(8,128)(2,1)}, bf16[4,128,240]{2,1,0:T(8,128)(2,1)}) custom-call(bf16[4,160,240]{2,1,0:T(8,128)(2,1)} %bitcast.694, bf16[4,160,120]{2,1,0:T(8,128)(2,1)} %bitcast.705, bf16[4,128,240]{2,1,0:T(8,128)(2,1)} %bitcast.695), custom_call_target="tpu_custom_call" | custom-call | tf_op jit(solution)/shard_map/pallas_call | solution.py:158
  654.8 39.0 %psum.7 = f32[2,960]{1,0:T(2,128)S(1)} all-reduce(f32[2,960]{1,0:T(2,128)S(1)} %pad_maximum_fusion.8), channel_id=1, replica_groups=mesh['dp'=8,'shard'=4] {'dp','shard'}, use_global_device_ids=true, to_apply=%region_36.38 | all-reduce | flops 1920 | bytes 15360 | tf_op jit(solution)/shard_map/psum | solution.py:458
  (379 shorter events, 113.8 us)
Async XLA Ops:
  7.2 124.9 %all-gather.4.cloned.1.call-start = ((), (), s32[]{:S(2)}) async-start(), calls=%async_computation.5 | async-start | bytes 1474560 | tf_op jit(solution)/shard_map/all_gather | solution.py:318
  9.4 41.2 %copy-start.7 = (f32[128,4,240]{2,0,1:T(8,128)}, f32[128,4,240]{2,0,1:T(8,128)S(1)}, u32[]{:S(2)}) copy-start(f32[128,4,240]{2,0,1:T(8,128)S(1)} %copy.313) | copy-start | bytes 1474564
  17.7 33.9 %copy-start.38 = (bf16[4,128,240]{2,1,0:T(8,128)(2,1)S(1)}, bf16[4,128,240]{2,1,0:T(8,128)(2,1)}, u32[]{:S(2)}) copy-start(bf16[4,128,240]{2,1,0:T(8,128)(2,1)} %shard_map.354) | copy-start | bytes 737284
  81.6 110.9 %all-gather.6.cloned.1.call-start = ((), (), s32[]{:S(2)}) async-start(), calls=%async_computation.6 | async-start | bytes 2949120 | tf_op jit(solution)/shard_map/all_gather | solution.py:259
  93.9 134.7 %all-gather.8.cloned.1.call-start = ((), (), s32[]{:S(2)}) async-start(), calls=%async_computation.7 | async-start | bytes 1382400 | tf_op jit(solution)/shard_map/all_gather | solution.py:260
  94.8 284.9 %reduce-scatter.10.cloned.1.call-start = ((), (), s32[]{:S(2)}) async-start(), calls=%async_computation.9 | async-start | bytes 1474560 | tf_op jit(solution)/shard_map/reduce_scatter | solution.py:211
  96.8 34.2 %copy-start.72 = (f32[128]{0:T(128)}, f32[128]{0:T(128)S(1)}, u32[]{:S(2)}) copy-start(f32[128]{0:T(128)S(1)} %fusion.126) | copy-start | bytes 1540
  97.4 33.4 %copy-start.46 = (bf16[1,128,960]{1,2,0:T(8,128)(2,1)S(1)}, bf16[1,128,960]{1,2,0:T(8,128)(2,1)}, u32[]{:S(2)}) copy-start(bf16[1,128,960]{1,2,0:T(8,128)(2,1)} %param.22) | copy-start | bytes 737284
  165.7 26.7 %copy-start.62 = (f32[3,128]{1,0:T(4,128)S(1)}, f32[3,128]{1,0:T(4,128)}, u32[]{:S(2)}) copy-start(f32[3,128]{1,0:T(4,128)} %copy-done.61) | copy-start | bytes 4612
  165.7 26.8 %copy-start.64 = (f32[3,128]{1,0:T(4,128)S(1)}, f32[3,128]{1,0:T(4,128)}, u32[]{:S(2)}) copy-start(f32[3,128]{1,0:T(4,128)} %copy-done.63) | copy-start | bytes 4612
  165.9 105.6 %copy-start.70 = (f32[128]{0:T(128)}, f32[128]{0:T(128)S(1)}, u32[]{:S(2)}) copy-start(f32[128]{0:T(128)S(1)} %get-tuple-element.230) | copy-start | bytes 1540
  165.9 105.6 %copy-start.77 = (f32[128]{0:T(128)}, f32[128]{0:T(128)S(1)}, u32[]{:S(2)}) copy-start(f32[128]{0:T(128)S(1)} %get-tuple-element.229) | copy-start | bytes 1540
  315.9 126.0 %reduce-scatter.14.cloned.1.call-start = ((), (), s32[]{:S(2)}) async-start(), calls=%async_computation.11 | async-start | bytes 552960 | tf_op jit(solution)/shard_map/reduce_scatter | solution.py:211
  318.4 188.2 %reduce-scatter.16.cloned.1.call-start = ((), (), s32[]{:S(2)}) async-start(), calls=%async_computation.12 | async-start | bytes 1382400
  321.7 244.5 %reduce-scatter.12.cloned.1.call-start = ((), (), s32[]{:S(2)}) async-start(), calls=%async_computation.10 | async-start | bytes 921600 | tf_op jit(solution)/shard_map/reduce_scatter | solution.py:211
  405.7 234.0 %reduce-scatter.8.cloned.1.call-start = ((), (), s32[]{:S(2)}) async-start(), calls=%async_computation.8 | async-start | bytes 2949120 | tf_op jit(solution)/shard_map/reduce_scatter | solution.py:211
  410.8 31.1 %copy-start.36 = (f32[240,120]{0,1:T(8,128)S(1)}, f32[240,120]{0,1:T(8,128)}, u32[]{:S(2)}) copy-start(f32[240,120]{0,1:T(8,128)} %copy-done.35) | copy-start | bytes 345604
  412.5 95.8 %copy-start.27 = (bf16[1600,240]{1,0:T(8,128)(2,1)S(1)}, bf16[1600,240]{1,0:T(8,128)(2,1)}, u32[]{:S(2)}) copy-start(bf16[1600,240]{1,0:T(8,128)(2,1)} %copy-done.26) | copy-start | bytes 2304004
  508.4 57.9 %copy-start.41 = (f32[240,200]{0,1:T(8,128)S(1)}, f32[240,200]{0,1:T(8,128)}, u32[]{:S(2)}) copy-start(f32[240,200]{0,1:T(8,128)} %param.25) | copy-start | bytes 576004
  508.4 57.9 %copy-start.49 = (f32[240,200]{0,1:T(8,128)S(1)}, f32[240,200]{0,1:T(8,128)}, u32[]{:S(2)}) copy-start(f32[240,200]{0,1:T(8,128)} %param.27) | copy-start | bytes 576004
  508.4 57.9 %copy-start.50 = (f32[240,200]{0,1:T(8,128)S(1)}, f32[240,200]{0,1:T(8,128)}, u32[]{:S(2)}) copy-start(f32[240,200]{0,1:T(8,128)} %param.26) | copy-start | bytes 576004
  568.0 84.4 %copy-start.8 = (f32[128,4,240]{2,0,1:T(8,128)S(1)}, f32[128,4,240]{2,0,1:T(8,128)}, u32[]{:S(2)}) copy-start(f32[128,4,240]{2,0,1:T(8,128)} %copy-done.7) | copy-start | bytes 1474564
  568.0 84.4 %copy-start.76 = (f32[128]{0:T(128)S(1)}, f32[128]{0:T(128)}, u32[]{:S(2)}) copy-start(f32[128]{0:T(128)} %copy-done.75) | copy-start | bytes 1540
  652.4 41.3 %copy-start.43 = (bf16[4,160,240]{2,1,0:T(8,128)(2,1)S(1)}, bf16[4,160,240]{2,1,0:T(8,128)(2,1)}, u32[]{:S(2)}) copy-start(bf16[4,160,240]{2,1,0:T(8,128)(2,1)} %get-tuple-element.39) | copy-start | bytes 921604
  (74 other events, 308.9 us)
Sparse Core Ops, SparseCore 0:
  81.7 46.1 all-gather.3
  130.6 55.0 all-gather.5
  188.5 39.9 all-gather.7
  316.0 63.5 reduce-scatter.9
  383.4 58.4 reduce-scatter.13
  445.2 61.3 reduce-scatter.15
  510.0 56.1 reduce-scatter.11
  570.1 69.5 reduce-scatter.7
